TPU v7x, 128 devices: a whole 4x4x4 slice. The times are simulated.
128 devices in a mesh: gx: 16 (over z, y), gy: 8 (over x, core).
Axes of the slice: x: 4, y: 4, z: 4, core: 2. Of those that a mesh axis runs over, the one named last changes fastest.
Arguments:
- x_tokens: bfloat16 [4096, 1024], P(('gx', 'gy')), may hold values from -6 to 6
- dy_tokens: bfloat16 [1024, 16384], P(None, ('gx', 'gy')), may hold values from -0.03125 to 0.03125
- samples: int32 [256], replicated, may hold values from 0 to 1023
- grad_acc: float32 [4096, 16384], P(('gx', 'gy')), may hold values from -0.625 to 0.625
- owners: int32 [8, 32], replicated, may hold values from 0 to 7, as said below
- left_stats: float32 [128, 4, 512, 512], P(('gx', 'gy')), may hold values from -1 to 5
- right_stats: float32 [128, 4, 512, 512], P(('gx', 'gy')), may hold values from -1 to 5
- left_roots: bfloat16 [128, 4, 512, 512], P(('gx', 'gy')), may hold values from -1 to 3
- right_roots: bfloat16 [128, 4, 512, 512], P(('gx', 'gy')), may hold values from -1 to 3
Outputs:
- update: float32 [4096, 16384], P(('gx', 'gy'))
- new_left_stats: float32 [128, 4, 512, 512], P(('gx', 'gy'))
- new_right_stats: float32 [128, 4, 512, 512], P(('gx', 'gy'))
Inputs may be any that keep to these rules, and one draw needn't show every extreme that they name: owners[r, c] is the gy index of the device that owns block (r, c) among the devices whose gx index is c // 2. The 2 blocks of one row r inside one column group have different owners; no device owns more than 4 blocks, and in every draw some device owns exactly 4. Slots past a device's count of blocks hold no block.
All inputs are finite; a program needn't handle non-finite values.
Results may differ from a plain program's by a relative error of at most 0.0041.
Values may be sent and summed in bfloat16 or wider, within the bound.
A program may use at most 128 MiB of HBM per device.

v0:
```python
import jax
import jax.numpy as jnp
from jax import lax
from jax.sharding import PartitionSpec as P

BLK = 512
BCOL = 2
SLOTS = 4


BETA_TWO = 0.9
EPSILON = 1e-06


def block_step(grad_block, left_stat, right_stat, left_root, right_root):
    highest = lax.Precision.HIGHEST
    gram_left = jnp.dot(
        grad_block, grad_block.T, precision=highest, preferred_element_type=jnp.float32
    )
    gram_right = jnp.dot(
        grad_block.T, grad_block, precision=highest, preferred_element_type=jnp.float32
    )
    new_left = BETA_TWO * left_stat + (1.0 - BETA_TWO) * gram_left
    new_right = BETA_TWO * right_stat + (1.0 - BETA_TWO) * gram_right
    narrow = grad_block.astype(jnp.bfloat16)
    half_product = jnp.dot(left_root, narrow, preferred_element_type=jnp.float32).astype(
        jnp.bfloat16
    )
    direction = jnp.dot(half_product, right_root, preferred_element_type=jnp.float32)
    scaled = direction * lax.rsqrt(jnp.mean(direction * direction) + EPSILON)
    return (new_left, new_right, scaled)


def slot_ranks(listed):
    entry_count = listed.shape[-1]
    places = jnp.arange(entry_count)
    same_owner = listed[..., :, None] == listed[..., None, :]
    earlier = places[None, :] < places[:, None]
    return jnp.sum(jnp.where(same_owner & earlier, 1, 0), axis=-1).astype(jnp.int32)


def body(
    x_tokens, dy_tokens, samples, grad_acc, owners, left_stats, right_stats, left_roots, right_roots
):
    rows_dev, col_count = grad_acc.shape
    across = lax.axis_size("gx")
    owner_count = lax.axis_size("gy")
    fold_count = across // owner_count
    tile_cols = BCOL * BLK
    column = lax.axis_index("gx")
    myself = lax.axis_index("gy")
    picked_inputs = jnp.take(x_tokens, samples, axis=1)
    picked_cotangents = jnp.take(dy_tokens, samples, axis=0)
    product = jnp.dot(
        picked_inputs,
        lax.all_gather(picked_cotangents, ("gx", "gy"), axis=1, tiled=True),
        preferred_element_type=jnp.float32,
    )
    gradient = grad_acc + product
    group_owners = lax.dynamic_slice_in_dim(owners, column * BCOL, BCOL, 1)
    listed = group_owners.reshape(-1)
    slot_rank = slot_ranks(listed)
    entries = listed.shape[0]
    places = jnp.arange(entries)
    slot_ids = jnp.arange(SLOTS)
    targets = jnp.arange(owner_count)
    owned_here = (listed == myself)[None, :] & (slot_rank[None, :] == slot_ids[:, None])
    occupied = jnp.any(owned_here, axis=1)
    shaped = gradient.reshape(1, 1, rows_dev, col_count)
    tile_rows = lax.all_to_all(
        lax.all_to_all(shaped.astype(jnp.bfloat16), "gx", split_axis=3, concat_axis=0, tiled=True),
        "gy",
        split_axis=0,
        concat_axis=2,
        tiled=True,
    ).astype(shaped.dtype)
    tile_blocks = tile_rows.reshape(BLK, BCOL, BLK)
    tile_owners = lax.dynamic_index_in_dim(group_owners, myself, 0, keepdims=False)
    outgoing = jnp.zeros((owner_count, BLK, BLK), jnp.float32)
    for block_index in range(BCOL):
        chosen = (tile_owners[block_index] == targets)[:, None, None]
        outgoing = outgoing + jnp.where(chosen, tile_blocks[None, :, block_index, :], 0.0)
    received = lax.all_to_all(
        outgoing.astype(jnp.bfloat16), "gy", split_axis=0, concat_axis=0, tiled=True
    ).astype(outgoing.dtype)
    sources = jnp.sum(jnp.where(owned_here, (places // BCOL)[None, :], 0), axis=1)
    grad_blocks = jnp.take(received, sources, axis=0)
    new_left, new_right, directions = jax.vmap(block_step)(
        grad_blocks, left_stats[0], right_stats[0], left_roots[0], right_roots[0]
    )
    keep_mask = occupied[:, None, None]
    left_out = jnp.where(keep_mask, new_left, left_stats[0])[None]
    right_out = jnp.where(keep_mask, new_right, right_stats[0])[None]
    returning = jnp.zeros((owner_count, BLK, BLK), jnp.float32)
    for slot_index in range(SLOTS):
        chosen = (occupied[slot_index] & (sources[slot_index] == targets))[:, None, None]
        returning = returning + jnp.where(chosen, directions[slot_index][None], 0.0)
    returned = lax.all_to_all(returning, "gy", split_axis=0, concat_axis=0, tiled=True)
    tile_update = jnp.take(returned, tile_owners, axis=0)
    tile_update = tile_update.transpose(1, 0, 2).reshape(
        fold_count, 1, owner_count * rows_dev, tile_cols
    )
    strips = lax.all_to_all(tile_update, "gy", split_axis=2, concat_axis=0, tiled=True)
    reassembled = lax.all_to_all(strips, "gx", split_axis=0, concat_axis=3, tiled=True)
    update = reassembled.reshape(rows_dev, col_count)
    return (update, left_out, right_out)


def solution(mesh):
    in_specs = (
        P(("gx", "gy"), None),
        P(None, ("gx", "gy")),
        P(),
        P(("gx", "gy"), None),
        P(),
        P(("gx", "gy"), None, None, None),
        P(("gx", "gy"), None, None, None),
        P(("gx", "gy"), None, None, None),
        P(("gx", "gy"), None, None, None),
    )
    out_specs = (
        P(("gx", "gy"), None),
        P(("gx", "gy"), None, None, None),
        P(("gx", "gy"), None, None, None),
    )
    return jax.shard_map(body, mesh=mesh, in_specs=in_specs, out_specs=out_specs, check_vma=False)
```

profile of v0, /device:TPU:1, one launch (start us, length us, event | category | flops | bytes accessed | tf_op | source)
XLA Modules:
  0.0 567.1 jit_solution(18230844967152191276)
XLA Ops:
  13.1 81.2 %all-gather.2.cloned.1.call-done = bf16[256,16384]{1,0:T(8,128)(2,1)} async-done(((bf16[256,128]{1,0:T(8,128)(2,1)}), bf16[256,16384]{1,0:T(8,128)(2,1)}) %all-gather.2.cloned.1.call-update) | async-done | bytes 8388624 | tf_op jit(solution)/shard_map/all_gather | solution.py:56
  94.3 5.6 fusion.1
  100.0 12.7 %copy.66 = bf16[1,1,32,16384]{2,1,0,3:T(2,128)(2,1)} copy(bf16[1,1,32,16384]{3,2,1,0:T(8,128)(2,1)S(1)} %fusion.1) | data formatting | bytes 2097152 | tf_op jit(solution)/shard_map/convert_element_type | solution.py:71
  113.2 90.8 %reduce = bf16[16384,32]{1,0:T(8,128)(2,1)} reduce(bf16[16384,1,1,32]{3,2,1,0:T(2,128)(2,1)} %bitcast.108, bf16[]{:T(256)} %broadcast.211), dimensions={1,2}, to_apply=%bitcast.101.reduce_sub_computation | reduce | bytes 2097154
  204.0 6.7 %reshape.184 = bf16[16,2,16384]{2,1,0:T(2,128)(2,1)S(1)} reshape(bf16[16384,32]{1,0:T(8,128)(2,1)} %reduce) | data formatting | bytes 2097152
  210.7 22.3 %all_to_all.70 = bf16[16,2,16384]{2,1,0:T(2,128)(2,1)} all-to-all(bf16[16,2,16384]{2,1,0:T(2,128)(2,1)S(1)} %reshape.184), channel_id=1, replica_groups=mesh['gx'=16,'gy'=8] {'gx'}, dimensions={0} | all-to-all | bytes 2097152 | tf_op jit(solution)/shard_map/all_to_all | solution.py:71
  233.0 11.4 %reshape.185 = bf16[16384,1,1,32]{3,2,1,0:T(2,128)(2,1)} reshape(bf16[16,2,16384]{2,1,0:T(2,128)(2,1)} %all_to_all.70) | data formatting | bytes 2097152
  244.4 15.1 %copy.67 = bf16[1,1,32,16384]{3,2,1,0:T(8,128)(2,1)S(1)} copy(bf16[1,1,32,16384]{2,1,0,3:T(2,128)(2,1)} %bitcast.109) | data formatting | bytes 2097152 | tf_op jit(solution)/shard_map/all_to_all | solution.py:71
  261.7 5.3 all-to-all-start.1
  269.0 13.1 %all-to-all-done.1 = bf16[16,1,32,1024]{3,2,1,0:T(8,128)(2,1)S(1)} async-done(((bf16[16,1,32,1024]{3,2,1,0:T(8,128)(2,1)}), bf16[16,1,32,1024]{3,2,1,0:T(8,128)(2,1)S(1)}, u32[]{:S(2)}, u32[]{:S(2)}) %all-to-all-start.1) | async-done | bytes 1048608 | tf_op jit(solution)/shard_map/all_to_all | solution.py:70
  295.4 5.3 all-to-all-start.2
  307.6 42.1 %all-to-all-done.2 = bf16[8,512,512]{2,1,0:T(8,128)(2,1)} async-done(((bf16[8,512,512]{2,1,0:T(8,128)(2,1)}), bf16[8,512,512]{2,1,0:T(8,128)(2,1)}, u32[]{:S(2)}, u32[]{:S(2)}) %all-to-all-start.2) | async-done | bytes 4194336 | tf_op jit(solution)/shard_map/all_to_all | solution.py:83
  349.7 6.6 %convert_element_type.41 = f32[8,512,512]{2,1,0:T(8,128)} convert(bf16[8,512,512]{2,1,0:T(8,128)(2,1)} %all-to-all-done.2) | non-fusion elementwise | flops 2097152 | bytes 12582912 | tf_op jit(solution)/shard_map/convert_element_type | solution.py:85
  356.2 6.2 %gather_fusion.2 = f32[4,512,512]{2,1,0:T(8,128)} fusion(f32[8,512,512]{2,1,0:T(8,128)} %convert_element_type.41, s32[1024]{0:T(1024)S(1)} %pad_clamp_fusion.1), kind=kCustom, calls=%fused_computation.2 | custom fusion | bytes 8388624 | tf_op jit(solution)/shard_map/jit(_take)/gather | solution.py:87
  362.4 7.6 %multiply_reduce_fusion = (f32[4]{0:T(128)S(1)}, f32[4,512,512]{2,1,0:T(8,128)}) fusion(bf16[1,4,512,512]{3,2,1,0:T(8,128)(2,1)S(1)} %copy-done, bf16[1,4,512,512]{3,2,1,0:T(8,128)(2,1)} %param.16, f32[4,512,512]{2,1,0:T(8,128)} %gather_fusion.2, pred[4]{0:T(512)(128)(4,1)S(1)} %compare_and_fusion.4), kind=kOutput, calls=%fused_computation.17 | convolution fusion | flops 2151677952 | bytes 12582932 | tf_op jit(solution)/shard_map/vmap()/dot_general | solution.py:29
  373.5 4.7 select_add_fusion
  378.2 6.0 %all-to-all-start.3 = ((f32[8,512,512]{2,1,0:T(8,128)}), f32[8,512,512]{2,1,0:T(8,128)}, u32[]{:S(2)}, u32[]{:S(2)}) async-start(f32[8,512,512]{2,1,0:T(8,128)} %select_add_fusion), calls=%async_computation.3 | async-start | bytes 16777216 | tf_op jit(solution)/shard_map/all_to_all | solution.py:98
  384.2 93.8 %all-to-all-done.3 = f32[8,512,512]{2,1,0:T(8,128)} async-done(((f32[8,512,512]{2,1,0:T(8,128)}), f32[8,512,512]{2,1,0:T(8,128)}, u32[]{:S(2)}, u32[]{:S(2)}) %all-to-all-start.3) | async-done | bytes 8388640 | tf_op jit(solution)/shard_map/all_to_all | solution.py:98
  478.0 4.1 gather_fusion.3
  490.0 29.8 %all_to_all.71 = f32[2,1,256,1024]{3,0,1,2:T(2,128)S(1)} all-to-all(f32[2,1,256,1024]{3,0,1,2:T(2,128)S(1)} %copy.74), channel_id=1, replica_groups=mesh['gx'=16,'gy'=8] {'gy'}, dimensions={2} | all-to-all | bytes 4194304 | tf_op jit(solution)/shard_map/all_to_all | solution.py:103
  522.1 4.4 all-to-all-start.5
  526.5 14.4 %fusion.3 = f32[1,4,512,512]{3,2,1,0:T(8,128)} fusion(f32[1,4,512,512]{3,2,1,0:T(8,128)} %param.15, pred[4]{0:T(512)(128)(4,1)S(1)} %fusion.34, f32[4,512,512]{2,1,0:T(8,128)} %gather_fusion.2, pred[4]{0:T(512)(128)(4,1)S(1)} %compare_and_fusion.4), kind=kOutput, calls=%fused_computation.12 | convolution fusion | flops 6447693824 | bytes 12582920 | tf_op jit(solution)/shard_map/vmap()/dot_general | solution.py:20
  541.0 9.2 %fusion.5 = f32[1,4,512,512]{3,2,1,0:T(8,128)} fusion(f32[1,4,512,512]{3,2,1,0:T(8,128)S(1)} %copy-done.3, pred[4]{0:T(512)(128)(4,1)S(1)} %fusion.34, f32[4,512,512]{2,1,0:T(8,128)S(1)} %copy-done.2, pred[4]{0:T(512)(128)(4,1)S(1)} %compare_and_fusion.4), kind=kOutput, calls=%fused_computation.16 | convolution fusion | flops 6447693824 | bytes 12582920 | tf_op jit(solution)/shard_map/vmap()/dot_general | solution.py:17
  550.1 6.6 %all-to-all-done.5 = f32[16,1,32,1024]{3,2,1,0:T(8,128)} async-done(((f32[16,1,32,1024]{3,2,1,0:T(8,128)}), f32[16,1,32,1024]{3,2,1,0:T(8,128)}, u32[]{:S(2)}, u32[]{:S(2)}) %all-to-all-start.5) | async-done | bytes 2097184 | tf_op jit(solution)/shard_map/all_to_all | solution.py:104
  (57 shorter events, 47.5 us)
Async XLA Ops:
  7.2 355.3 %copy-start = (bf16[1,4,512,512]{3,2,1,0:T(8,128)(2,1)S(1)}, bf16[1,4,512,512]{3,2,1,0:T(8,128)(2,1)}, u32[]{:S(2)}) copy-start(bf16[1,4,512,512]{3,2,1,0:T(8,128)(2,1)} %param.17) | copy-start | bytes 6291460
  7.2 87.1 %all-gather.2.cloned.1.call-start = ((), (), s32[]{:S(2)}) async-start(), calls=%async_computation.6 | async-start | bytes 8454144 | tf_op jit(solution)/shard_map/all_gather | solution.py:56
  259.5 7.5 %copy-start.4 = (s32[8,32]{1,0:T(8,128)S(1)}, s32[8,32]{1,0:T(8,128)}, u32[]{:S(2)}) copy-start(s32[8,32]{1,0:T(8,128)} %param.13) | copy-start | bytes 3076
  261.7 20.4 %all-to-all-start.1 = ((bf16[16,1,32,1024]{3,2,1,0:T(8,128)(2,1)}), bf16[16,1,32,1024]{3,2,1,0:T(8,128)(2,1)S(1)}, u32[]{:S(2)}, u32[]{:S(2)}) async-start(bf16[16,1,32,1024]{3,2,1,0:T(8,128)(2,1)} %copy.68), calls=%async_computation.1 | async-start | bytes 2097152 | tf_op jit(solution)/shard_map/all_to_all | solution.py:70
  295.4 54.3 %all-to-all-start.2 = ((bf16[8,512,512]{2,1,0:T(8,128)(2,1)}), bf16[8,512,512]{2,1,0:T(8,128)(2,1)}, u32[]{:S(2)}, u32[]{:S(2)}) async-start(bf16[8,512,512]{2,1,0:T(8,128)(2,1)} %add_convert_fusion), calls=%async_computation.2 | async-start | bytes 8388608 | tf_op jit(solution)/shard_map/all_to_all | solution.py:83
  378.2 99.8 %all-to-all-start.3 = ((f32[8,512,512]{2,1,0:T(8,128)}), f32[8,512,512]{2,1,0:T(8,128)}, u32[]{:S(2)}, u32[]{:S(2)}) async-start(f32[8,512,512]{2,1,0:T(8,128)} %select_add_fusion), calls=%async_computation.3 | async-start | bytes 16777216 | tf_op jit(solution)/shard_map/all_to_all | solution.py:98
  522.1 34.7 %all-to-all-start.5 = ((f32[16,1,32,1024]{3,2,1,0:T(8,128)}), f32[16,1,32,1024]{3,2,1,0:T(8,128)}, u32[]{:S(2)}, u32[]{:S(2)}) async-start(f32[16,1,32,1024]{3,2,1,0:T(8,128)} %bitcast.31), calls=%async_computation.5 | async-start | bytes 4194304 | tf_op jit(solution)/shard_map/all_to_all | solution.py:104
  526.5 14.4 %copy-start.2 = (f32[4,512,512]{2,1,0:T(8,128)S(1)}, f32[4,512,512]{2,1,0:T(8,128)}, u32[]{:S(2)}) copy-start(f32[4,512,512]{2,1,0:T(8,128)} %gather_fusion.2) | copy-start | bytes 12582916
  526.5 14.4 %copy-start.3 = (f32[1,4,512,512]{3,2,1,0:T(8,128)S(1)}, f32[1,4,512,512]{3,2,1,0:T(8,128)}, u32[]{:S(2)}) copy-start(f32[1,4,512,512]{3,2,1,0:T(8,128)} %param.14) | copy-start | bytes 12582916
  540.9 19.0 %copy-start.1 = (bf16[1,4,512,512]{3,2,1,0:T(8,128)(2,1)S(1)}, bf16[1,4,512,512]{3,2,1,0:T(8,128)(2,1)}, u32[]{:S(2)}) copy-start(bf16[1,4,512,512]{3,2,1,0:T(8,128)(2,1)} %param.17) | copy-start | bytes 6291460
Sparse Core Ops, SparseCore 0:
  11.4 82.8 all-gather.1
where the time goes:
time: 578 us; the launch traced here: 567 us
  waiting for transfers between devices  237 us (41%)
  other arithmetic  118 us (20%)
  local copies, waits for them, and re-layouts  87.6 us (15%)
  blocking collectives  52.1 us (9%)
  matrix products  36.8 us (6%)
  starting transfers between devices  21.1 us (4%)
  between operations  14.7 us (3%)
    all_to_all x1, waiting for transfers between devices, body(): lax.all_to_all(returning, 'gy', split_axis=0, concat_axis=0, tiled=True)  93.8 us
    unnamed x1, other arithmetic  90.8 us
    all_gather x1, waiting for transfers between devices, body(): lax.all_gather(picked_cotangents, ('gx', 'gy'), axis=1, tiled=True)  81.2 us
    all_to_all x1, waiting for transfers between devices, body(): lax.all_to_all(outgoing.astype(jnp.bfloat16), 'gy', split_axis=0, concat_...  42.1 us
    all_to_all x1, blocking collectives, body(): lax.all_to_all(tile_update, 'gy', split_axis=2, concat_axis=0, tiled=True)  29.8 us
    unnamed x17, local copies, waits for them, and re-layouts  23.6 us
    all_to_all x1, blocking collectives, body(): lax.all_to_all(shaped.astype(jnp.bfloat16), 'gx', split_axis=3, concat_ax...  22.3 us
    all_to_all x2, local copies, waits for them, and re-layouts, body(): lax.all_to_all(shaped.astype(jnp.bfloat16), 'gx', split_axis=3, concat_ax...  16.7 us
  transfers between devices with their start and end apart: 5, of which 5 were waited for; matrix products, arithmetic and copies ran while one was open for 6% of the time, Pallas kernels for 0%

commit v1 on v0

v1 whole, which is shorter than its diff:
```python
import functools

import jax
import jax.numpy as jnp
from jax import lax
from jax.experimental import pallas as pl
from jax.experimental.pallas import tpu as pltpu
from jax.sharding import PartitionSpec as P

BCOL = 2
SLOTS = 4
BETA_TWO = 0.9
EPSILON = 1e-06
CHUNKS = 4

MESH = pl.DeviceIdType.MESH
F32 = jnp.float32
BF16 = jnp.bfloat16


def exchange_kernel(
    nx, ny, q_count,
    x_ref, dy_ref, samples_ref, grad_ref, owners_ref, lroot_ref, rroot_ref,
    rows_out, grad_out,
    *scratch,
):
    names = iter(scratch)

    def several(count):
        return [next(names) for _ in range(count)]

    acc = several(q_count)
    mine = several(q_count)
    pack = several(q_count)
    held = several(q_count)
    send = several(q_count)
    back = several(q_count)
    strips = several(q_count)
    xs, dys, lroot, rroot, half, direction, source_tab, key_tab = several(8)
    (x_send, x_recv, dy_send, dy_recv, root_sem, keep_sem,
     a_send, a_recv, b_send, b_recv, c_send, c_recv, d_send, d_recv) = several(14)

    me_x, me_y = lax.axis_index("gx"), lax.axis_index("gy")
    fold = nx // ny
    rows = grad_ref.shape[0]
    blk = fold * ny * rows
    w = blk // q_count
    br = ny
    tile = BCOL * blk
    dcols = dy_ref.shape[1]
    entries = br * BCOL

    def peer_x(d):
        return lax.rem(me_x + d, nx)

    def peer_y(d):
        return lax.rem(me_y + d, ny)

    barrier = pltpu.get_barrier_semaphore()

    def greet_x(d, _):
        pl.semaphore_signal(barrier, inc=1, device_id=(peer_x(d), me_y), device_id_type=MESH)
        return 0

    def greet_y(d, _):
        pl.semaphore_signal(barrier, inc=1, device_id=(me_x, peer_y(d)), device_id_type=MESH)
        return 0

    lax.fori_loop(1, nx, greet_x, 0)
    lax.fori_loop(1, ny, greet_y, 0)

    roots = [
        pltpu.make_async_copy(lroot_ref, lroot, root_sem.at[0]),
        pltpu.make_async_copy(rroot_ref, rroot, root_sem.at[1]),
    ]
    for copy in roots:
        copy.start()
    pool = x_ref.shape[1]
    count = samples_ref.shape[1]
    chosen = (lax.broadcasted_iota(jnp.int32, (pool, count), 0) == samples_ref[...])
    chosen = jnp.where(chosen, 1.0, 0.0).astype(BF16)
    xs[pl.ds(me_x, 1)] = jnp.dot(x_ref[...], chosen, preferred_element_type=F32).astype(BF16)[None]
    my_cols = pl.ds(pl.multiple_of(me_y * dcols, dcols), dcols)
    dys[:, my_cols] = lax.dot_general(
        chosen, dy_ref[...], (((0,), (0,)), ((), ())), preferred_element_type=F32
    ).astype(BF16)

    pl.semaphore_wait(barrier, nx + ny - 2)

    def send_x(d, _):
        pltpu.make_async_remote_copy(
            xs.at[me_x], xs.at[me_x], x_send, x_recv, (peer_x(d), me_y), MESH
        ).start()
        return 0

    def send_dy(d, _):
        pltpu.make_async_remote_copy(
            dys.at[:, my_cols], dys.at[:, my_cols], dy_send, dy_recv, (me_x, peer_y(d)), MESH
        ).start()
        return 0

    def acc_source(group, block, q):
        first = pl.multiple_of(group * tile + block * blk + q * w, 128)
        return grad_ref.at[:, pl.ds(first, w)]

    lax.fori_loop(1, ny, send_dy, 0)
    lax.fori_loop(1, nx, send_x, 0)
    for q in range(q_count):
        for block in range(BCOL):
            pltpu.make_async_copy(
                acc_source(me_x, block, q), acc[q].at[me_x, block], a_recv.at[q]
            ).start()

        def send_acc(d, _, q=q):
            for block in range(BCOL):
                pltpu.make_async_remote_copy(
                    acc_source(peer_x(d), block, q), acc[q].at[me_x, block],
                    a_send.at[q], a_recv.at[q], (peer_x(d), me_y), MESH,
                ).start()
            return 0

        lax.fori_loop(1, nx, send_acc, 0)

    keys = []
    listed = [owners_ref[e // BCOL, me_x * BCOL + e % BCOL] for e in range(entries)]
    for e in range(entries):
        rank = jnp.int32(0)
        for before in range(e):
            rank = rank + jnp.where(listed[before] == listed[e], 1, 0)
        keys.append(listed[e] * SLOTS + rank)
        key_tab[e] = keys[e]

    def find_source(k, _):
        place = jnp.int32(0)
        for e in range(entries):
            place = place + jnp.where(keys[e] == k, (e % BCOL) * br + e // BCOL, 0)
        source_tab[k] = place
        return 0

    lax.fori_loop(0, ny * SLOTS, find_source, 0)

    def landed(ref, sem):
        pltpu.make_async_copy(ref, ref, sem).wait()

    for q in range(q_count):
        if q == 0:
            landed(xs.at[pl.ds(0, nx - 1)], x_recv)
            landed(dys.at[:, pl.ds(0, (ny - 1) * dcols)], dy_recv)
        landed(acc[q], a_recv.at[q])
        for block in range(BCOL):
            first = block * blk + q * w
            product = jnp.dot(
                xs[...].reshape(nx * rows, count), dys[:, first:first + w],
                preferred_element_type=F32,
            ).reshape(nx, rows, w)
            total = (acc[q][:, block] + product).astype(BF16)
            mine[q][block * br:(block + 1) * br] = total.reshape(br, fold, rows, w)

        def fill(owner, _, q=q):
            for slot in range(SLOTS):
                pack[q][owner, slot] = mine[q][source_tab[owner * SLOTS + slot]]
            return 0

        lax.fori_loop(0, ny, fill, 0)
        pltpu.make_async_copy(pack[q].at[me_y], held[q].at[:, :, me_y], b_recv.at[q]).start()

        def send_block(d, _, q=q):
            pltpu.make_async_remote_copy(
                pack[q].at[peer_y(d)], held[q].at[:, :, me_y],
                b_send.at[q], b_recv.at[q], (me_x, peer_y(d)), MESH,
            ).start()
            return 0

        lax.fori_loop(1, ny, send_block, 0)

    for copy in roots:
        copy.wait()

    kept = []
    for q in range(q_count):
        landed(held[q], b_recv.at[q])
        kept.append(pltpu.make_async_copy(
            held[q], grad_out.at[:, :, :, :, pl.ds(q * w, w)], keep_sem.at[q]
        ))
        kept[q].start()

        def left(slot, _, q=q):
            half[slot, :, q * w:(q + 1) * w] = jnp.dot(
                lroot[slot], held[q][slot].reshape(blk, w), preferred_element_type=F32
            ).astype(BF16)
            return 0

        lax.fori_loop(0, SLOTS, left, 0)

    part = blk // 4

    def right(slot, _):
        squares = jnp.zeros((1, blk), F32)
        for p in range(4):
            product = jnp.dot(
                half[slot, p * part:(p + 1) * part, :], rroot[slot], preferred_element_type=F32
            )
            direction[p * part:(p + 1) * part, :] = product
            squares = squares + jnp.sum(product * product, axis=0, keepdims=True)
        scale = lax.rsqrt(jnp.sum(squares) / (blk * blk) + EPSILON)
        for q in range(q_count):
            scaled = (direction[:, q * w:(q + 1) * w] * scale).astype(BF16)
            send[q][slot] = scaled.reshape(fold, ny, rows, w)
        return 0

    lax.fori_loop(0, SLOTS, right, 0)

    my_slots = pl.ds(me_y * SLOTS, SLOTS)
    for q in range(q_count):
        pltpu.make_async_copy(send[q].at[:, :, me_y], back[q].at[my_slots], c_recv.at[q]).start()

        def send_back(d, _, q=q):
            pltpu.make_async_remote_copy(
                send[q].at[:, :, peer_y(d)], back[q].at[my_slots],
                c_send.at[q], c_recv.at[q], (me_x, peer_y(d)), MESH,
            ).start()
            return 0

        lax.fori_loop(1, ny, send_back, 0)

    for q in range(q_count):
        landed(back[q], c_recv.at[q])
        for e in range(entries):
            r, block = e // BCOL, e % BCOL
            strips[q][r * fold:(r + 1) * fold, block] = back[q][key_tab[e]]
        pltpu.make_async_copy(strips[q].at[me_x], rows_out.at[q, me_x], d_recv.at[q]).start()

        def send_rows(d, _, q=q):
            pltpu.make_async_remote_copy(
                strips[q].at[peer_x(d)], rows_out.at[q, me_x],
                d_send.at[q], d_recv.at[q], (peer_x(d), me_y), MESH,
            ).start()
            return 0

        lax.fori_loop(1, nx, send_rows, 0)

    for q in range(q_count):
        landed(rows_out.at[q], d_recv.at[q])
        kept[q].wait()
        landed(acc[q].at[pl.ds(0, nx - 1)], a_send.at[q])
        landed(pack[q].at[pl.ds(0, ny - 1)], b_send.at[q])
        landed(pack[q].at[pl.ds(0, ny - 1)], c_send.at[q])
        landed(strips[q].at[pl.ds(0, nx - 1)], d_send.at[q])
    landed(xs.at[pl.ds(0, nx - 1)], x_send)
    landed(dys.at[:, pl.ds(0, (ny - 1) * dcols)], dy_send)


def finish_kernel(
    owners_ref, grad_ref, left_ref, right_ref, rows_ref, update_ref, new_left_ref, new_right_ref
):
    me_x, me_y = lax.axis_index("gx"), lax.axis_index("gy")
    slot, part = pl.program_id(0), pl.program_id(1)
    owned = jnp.int32(0)
    for r in range(owners_ref.shape[0]):
        for c in range(BCOL):
            owned = owned + jnp.where(owners_ref[r, me_x * BCOL + c] == me_y, 1, 0)
    occupied = slot < owned
    old = jnp.where(occupied, BETA_TWO, 1.0)
    new = jnp.where(occupied, 1.0 - BETA_TWO, 0.0)
    span = left_ref.shape[1]
    first = pl.multiple_of(part * span, span)
    block = grad_ref[0]
    gram_left = lax.dot_general(
        grad_ref[0, pl.ds(first, span), :], block, (((1,), (1,)), ((), ())), preferred_element_type=F32
    )
    new_left_ref[0] = old * left_ref[0] + new * gram_left
    gram_right = lax.dot_general(
        grad_ref[0, :, pl.ds(first, span)], block, (((0,), (0,)), ((), ())), preferred_element_type=F32
    )
    new_right_ref[0] = old * right_ref[0] + new * gram_right
    q_count, groups, blocks, _, w = rows_ref.shape
    for group in range(groups):
        for b in range(blocks):
            for q in range(q_count):
                at = ((group * blocks + b) * q_count + q) * w
                update_ref[:, at:at + w] = rows_ref[q, group, b].astype(F32)


def body(
    x_tokens, dy_tokens, samples, grad_acc, owners, left_stats, right_stats, left_roots, right_roots
):
    nx, ny = lax.axis_size("gx"), lax.axis_size("gy")
    rows, cols = grad_acc.shape
    fold = nx // ny
    blk = left_stats.shape[-1]
    q_count = CHUNKS
    w = blk // q_count
    count = samples.shape[0]
    br = ny
    dcols = dy_tokens.shape[1]
    vmem, hbm = pl.BlockSpec(memory_space=pltpu.VMEM), pl.BlockSpec(memory_space=pl.ANY)
    smem = pl.BlockSpec(memory_space=pltpu.SMEM)

    def each(shape, dtype):
        return [pltpu.VMEM(shape, dtype) for _ in range(q_count)]

    dma = pltpu.SemaphoreType.DMA
    rows_back, grad = pl.pallas_call(
        functools.partial(exchange_kernel, nx, ny, q_count),
        out_shape=(
            jax.ShapeDtypeStruct((q_count, nx, BCOL, rows, w), BF16),
            jax.ShapeDtypeStruct((SLOTS, fold, ny, rows, blk), BF16),
        ),
        in_specs=[vmem, vmem, vmem, hbm, smem, hbm, hbm],
        out_specs=(hbm, hbm),
        scratch_shapes=[
            *each((nx, BCOL, rows, w), F32),
            *each((BCOL * br, fold, rows, w), BF16),
            *each((ny, SLOTS, fold, rows, w), BF16),
            *each((SLOTS, fold, ny, rows, w), BF16),
            *each((SLOTS, fold, ny, rows, w), BF16),
            *each((ny * SLOTS, fold, rows, w), BF16),
            *each((nx, BCOL, rows, w), BF16),
            pltpu.VMEM((nx, rows, count), BF16),
            pltpu.VMEM((count, ny * dcols), BF16),
            pltpu.VMEM((SLOTS, blk, blk), BF16),
            pltpu.VMEM((SLOTS, blk, blk), BF16),
            pltpu.VMEM((SLOTS, blk, blk), BF16),
            pltpu.VMEM((blk, blk), F32),
            pltpu.SMEM((ny * SLOTS,), jnp.int32),
            pltpu.SMEM((br * BCOL,), jnp.int32),
            dma, dma, dma, dma, dma((2,)), dma((q_count,)),
            *[dma((q_count,)) for _ in range(8)],
        ],
        compiler_params=pltpu.CompilerParams(
            collective_id=0, has_side_effects=True, vmem_limit_bytes=48 * 2**20
        ),
        name="exchange",
    )(
        x_tokens, dy_tokens, samples.reshape(1, count), grad_acc, owners,
        left_roots[0], right_roots[0],
    )
    parts = 2
    span = blk // parts
    steps = SLOTS * parts
    tall = pl.BlockSpec((1, span, blk), lambda s, p: (s, p, 0))
    update, new_left, new_right = pl.pallas_call(
        finish_kernel,
        grid=(SLOTS, parts),
        out_shape=(
            jax.ShapeDtypeStruct((rows, cols), F32),
            jax.ShapeDtypeStruct((SLOTS, blk, blk), F32),
            jax.ShapeDtypeStruct((SLOTS, blk, blk), F32),
        ),
        in_specs=[
            smem,
            pl.BlockSpec((1, blk, blk), lambda s, p: (s, 0, 0)),
            tall,
            tall,
            pl.BlockSpec(
                (q_count, nx // steps, BCOL, rows, w), lambda s, p: (0, s * parts + p, 0, 0, 0)
            ),
        ],
        out_specs=(
            pl.BlockSpec((rows, cols // steps), lambda s, p: (0, s * parts + p)),
            tall,
            tall,
        ),
        compiler_params=pltpu.CompilerParams(vmem_limit_bytes=48 * 2**20),
        name="finish",
    )(owners, grad.reshape(SLOTS, blk, blk), left_stats[0], right_stats[0], rows_back)
    return update, new_left[None], new_right[None]


def solution(mesh):
    split = P(("gx", "gy"), None)
    deep = P(("gx", "gy"), None, None, None)
    return jax.shard_map(
        body,
        mesh=mesh,
        in_specs=(split, P(None, ("gx", "gy")), P(), split, P(), deep, deep, deep, deep),
        out_specs=(split, deep, deep),
        check_vma=False,
    )
```

time: 578 us -> 97.7 us (0.17); the launches traced: 567 us -> 97.3 us
  waiting for transfers between devices: 237 us -> 0 us
  other arithmetic: 118 us -> 0 us
  Pallas kernels: 0 us -> 91.9 us
  local copies, waits for them, and re-layouts: 87.6 us -> 4.74 us
  blocking collectives: 52.1 us -> 0 us
  matrix products: 36.8 us -> 0 us
  starting transfers between devices: 21.1 us -> 0 us
  between operations: 14.7 us -> 0.65 us
    all_to_all x4 -> x0, waiting for transfers between devices: 156 us -> none  [the longest x1 93.8 us: body(): lax.all_to_all(returning, 'gy', split_axis=0, concat_axis=0, tiled=True)]
    pallas_call x0 -> x2, Pallas kernels: none -> 91.9 us  [the longest x1 81.2 us: body(): pl.pallas_call(functools.partial(exchange_kernel, nx, ny, q_count), out_s...]
    unnamed x1 -> x0, other arithmetic: 90.8 us -> none
    all_gather x1 -> x0, waiting for transfers between devices: 81.2 us -> none  [body(): lax.all_gather(picked_cotangents, ('gx', 'gy'), axis=1, tiled=True)]
    all_to_all x2 -> x0, blocking collectives: 52.1 us -> none  [the longest x1 29.8 us: body(): lax.all_to_all(tile_update, 'gy', split_axis=2, concat_axis=0, tiled=True)]
    dot_general x4 -> x0, matrix products: 36.8 us -> none  [the longest x1 14.4 us: block_step(): jnp.dot(grad_block.T, grad_block, precision=highest, preferred_element_ty...]
    all_to_all x4 -> x0, starting transfers between devices: 21 us -> none  [the longest x1 5.96 us: body(): lax.all_to_all(returning, 'gy', split_axis=0, concat_axis=0, tiled=True)]
    all_to_all x4 -> x0, local copies, waits for them, and re-layouts: 18.9 us -> none  [the longest x2 16.7 us: body(): lax.all_to_all(shaped.astype(jnp.bfloat16), 'gx', split_axis=3, concat_ax...]
  transfers between devices with their start and end apart: 5 -> 0, of which waited for: 5 -> 0; matrix products, arithmetic and copies ran while one was open for 6% -> 0% of each run, Pallas kernels for 0% -> 0%
where the time goes in v1:
time: 97.7 us; the launch traced here: 97.3 us
  Pallas kernels  91.9 us (94%)
  local copies, waits for them, and re-layouts  4.74 us (5%)
    pallas_call x1, Pallas kernels, body(): pl.pallas_call(functools.partial(exchange_kernel, nx, ny, q_count), out_s...  81.2 us
    pallas_call x1, Pallas kernels, body(): pl.pallas_call(finish_kernel, grid=(SLOTS, parts), out_shape=(jax.ShapeDt...  10.7 us
    unnamed x10, local copies, waits for them, and re-layouts  4.74 us

profile of v1, /device:TPU:1, one launch (start us, length us, event | category | flops | bytes accessed | tf_op | source)
XLA Modules:
  0.0 97.3 jit_solution(6742758450029453545)
XLA Ops:
  0.6 0.0 copy-start
  0.6 1.6 %copy-done = f32[32,16384]{1,0:T(8,128)S(1)} copy-done((f32[32,16384]{1,0:T(8,128)S(1)}, f32[32,16384]{1,0:T(8,128)}, u32[]{:S(2)}) %copy-start) | copy-done | bytes 2097176
  2.2 0.0 copy-start.1
  2.2 0.9 copy-done.1
  3.2 0.0 copy-start.2
  3.2 0.8 copy-done.2
  4.0 0.0 copy-start.3
  4.0 0.7 copy-done.3
  4.7 0.0 copy-start.4
  4.7 0.7 copy-done.4
  5.4 81.2 %exchange.1 = (bf16[4,16,2,32,128]{4,3,2,1,0:T(8,128)(2,1)S(1)}, bf16[4,2,8,32,512]{4,3,2,1,0:T(8,128)(2,1)S(1)}) custom-call(bf16[32,1024]{1,0:T(8,128)(2,1)S(1)} %copy-done.2, bf16[1024,128]{1,0:T(8,128)(2,1)S(1)} %copy-done.1, s32[1,256]{1,0:T(1,128)S(1)} %bitcast.9, f32[32,16384]{1,0:T(8,128)S(1)} %copy-done, s32[8,32]{1,0:T(8,128)S(1)} %copy-done.3, ...), custom_call_target="tpu_custom_call" | custom-call | tf_op jit(solution)/shard_map/exchange/pallas_call | solution.py:303
  86.6 10.7 %finish.1 = (f32[32,16384]{1,0:T(8,128)}, f32[4,512,512]{2,1,0:T(8,128)}, f32[4,512,512]{2,1,0:T(8,128)}) custom-call(s32[8,32]{1,0:T(8,128)S(1)} %copy-done.3, bf16[4,512,512]{2,1,0:T(8,128)(2,1)S(1)} %bitcast.8, f32[4,512,512]{2,1,0:T(8,128)} %bitcast.10, f32[4,512,512]{2,1,0:T(8,128)} %bitcast.11, bf16[4,16,2,32,128]{4,3,2,1,0:T(8,128)(2,1)S(1)} %get-tuple-element.9.rows_ref), custom_call_target="tpu_custom_call" | custom-call | tf_op jit(solution)/shard_map/finish/pallas_call | solution.py:342
Async XLA Ops:
  0.6 1.6 %copy-start = (f32[32,16384]{1,0:T(8,128)S(1)}, f32[32,16384]{1,0:T(8,128)}, u32[]{:S(2)}) copy-start(f32[32,16384]{1,0:T(8,128)} %grad_ref.1) | copy-start | bytes 6291460
  2.2 0.9 copy-start.1
  3.2 0.8 copy-start.2
  4.0 0.7 copy-start.3
  4.7 0.7 copy-start.4

commit v2 on v1

v2 whole, which is shorter than its diff:
```python
import functools

import jax
import jax.numpy as jnp
from jax import lax
from jax.experimental import pallas as pl
from jax.experimental.pallas import tpu as pltpu
from jax.sharding import PartitionSpec as P

BCOL = 2
SLOTS = 4
BETA_TWO = 0.9
EPSILON = 1e-06
CHUNKS = 4

MESH = pl.DeviceIdType.MESH
F32 = jnp.float32
BF16 = jnp.bfloat16


def exchange_kernel(
    nx, ny, q_count,
    x_hbm, dy_hbm, samples_hbm, grad_hbm, owners_hbm, left_hbm, right_hbm, lroot_hbm, rroot_hbm,
    rows_out, left_out, right_out,
    *scratch,
):
    names = iter(scratch)

    def several(count):
        return [next(names) for _ in range(count)]

    mine_rows = several(q_count)
    acc = several(q_count)
    mine = several(q_count)
    pack = several(q_count)
    send = several(q_count)
    back = several(q_count)
    strips = several(q_count)
    (held, xs, dys, lroot, rroot, half, direction, left, right,
     x_ref, dy_ref, samples_ref, grad_ref, owners_ref, source_tab, key_tab) = several(16)
    (in_sem, x_send, x_recv, dy_send, dy_recv, keep_sem,
     a_send, a_recv, b_send, b_recv, c_send, c_recv, d_send, d_recv) = several(14)

    me_x, me_y = lax.axis_index("gx"), lax.axis_index("gy")
    fold = nx // ny
    rows = grad_ref.shape[0]
    blk = fold * ny * rows
    w = blk // q_count
    br = ny
    tile = BCOL * blk
    dcols = dy_ref.shape[1]
    entries = br * BCOL

    def peer_x(d):
        return lax.rem(me_x + d, nx)

    def peer_y(d):
        return lax.rem(me_y + d, ny)

    barrier = pltpu.get_barrier_semaphore()

    def greet_x(d, _):
        pl.semaphore_signal(barrier, inc=1, device_id=(peer_x(d), me_y), device_id_type=MESH)
        return 0

    def greet_y(d, _):
        pl.semaphore_signal(barrier, inc=1, device_id=(me_x, peer_y(d)), device_id_type=MESH)
        return 0

    lax.fori_loop(1, nx, greet_x, 0)
    lax.fori_loop(1, ny, greet_y, 0)

    pairs = [
        (samples_hbm, samples_ref), (x_hbm, x_ref), (dy_hbm, dy_ref), (grad_hbm, grad_ref),
        (owners_hbm, owners_ref), (lroot_hbm, lroot), (rroot_hbm, rroot),
        (left_hbm, left), (right_hbm, right),
    ]
    loads = [pltpu.make_async_copy(a, b, in_sem.at[i]) for i, (a, b) in enumerate(pairs)]
    for load in loads:
        load.start()
    for load in loads[:3]:
        load.wait()
    pool = x_ref.shape[1]
    count = samples_ref.shape[1]
    chosen = (lax.broadcasted_iota(jnp.int32, (pool, count), 0) == samples_ref[...])
    chosen = jnp.where(chosen, 1.0, 0.0).astype(BF16)
    xs[pl.ds(me_x, 1)] = jnp.dot(x_ref[...], chosen, preferred_element_type=F32).astype(BF16)[None]
    my_cols = pl.ds(pl.multiple_of(me_y * dcols, dcols), dcols)
    dys[:, my_cols] = lax.dot_general(
        chosen, dy_ref[...], (((0,), (0,)), ((), ())), preferred_element_type=F32
    ).astype(BF16)
    loads[3].wait()

    def narrow(group, _):
        for q in range(q_count):
            for block in range(BCOL):
                first = pl.multiple_of(group * tile + block * blk + q * w, 128)
                mine_rows[q][group, block] = grad_ref[:, pl.ds(first, w)].astype(BF16)
        return 0

    lax.fori_loop(0, nx, narrow, 0)

    pl.semaphore_wait(barrier, nx + ny - 2)

    def send_x(d, _):
        pltpu.make_async_remote_copy(
            xs.at[me_x], xs.at[me_x], x_send, x_recv, (peer_x(d), me_y), MESH
        ).start()
        return 0

    def send_dy(d, _):
        pltpu.make_async_remote_copy(
            dys.at[:, my_cols], dys.at[:, my_cols], dy_send, dy_recv, (me_x, peer_y(d)), MESH
        ).start()
        return 0

    lax.fori_loop(1, ny, send_dy, 0)
    lax.fori_loop(1, nx, send_x, 0)
    for q in range(q_count):
        pltpu.make_async_copy(mine_rows[q].at[me_x], acc[q].at[me_x], a_recv.at[q]).start()

        def send_acc(d, _, q=q):
            pltpu.make_async_remote_copy(
                mine_rows[q].at[peer_x(d)], acc[q].at[me_x],
                a_send.at[q], a_recv.at[q], (peer_x(d), me_y), MESH,
            ).start()
            return 0

        lax.fori_loop(1, nx, send_acc, 0)

    loads[4].wait()
    keys = []
    owned = jnp.int32(0)
    listed = [owners_ref[e // BCOL, me_x * BCOL + e % BCOL] for e in range(entries)]
    for e in range(entries):
        rank = jnp.int32(0)
        for before in range(e):
            rank = rank + jnp.where(listed[before] == listed[e], 1, 0)
        keys.append(listed[e] * SLOTS + rank)
        key_tab[e] = keys[e]
        owned = owned + jnp.where(listed[e] == me_y, 1, 0)

    def find_source(k, _):
        place = jnp.int32(0)
        for e in range(entries):
            place = place + jnp.where(keys[e] == k, (e % BCOL) * br + e // BCOL, 0)
        source_tab[k] = place
        return 0

    lax.fori_loop(0, ny * SLOTS, find_source, 0)

    def landed(ref, sem):
        pltpu.make_async_copy(ref, ref, sem).wait()

    def chunk(q):
        return slice(q * w, (q + 1) * w)

    for q in range(q_count):
        if q == 0:
            landed(xs.at[pl.ds(0, nx - 1)], x_recv)
            landed(dys.at[:, pl.ds(0, (ny - 1) * dcols)], dy_recv)
        landed(acc[q], a_recv.at[q])
        for block in range(BCOL):
            first = block * blk + q * w
            product = jnp.dot(
                xs[...].reshape(nx * rows, count), dys[:, first:first + w],
                preferred_element_type=F32,
            ).reshape(nx, rows, w)
            total = (acc[q][:, block].astype(F32) + product).astype(BF16)
            mine[q][block * br:(block + 1) * br] = total.reshape(br, fold, rows, w)

        def fill(owner, _, q=q):
            for slot in range(SLOTS):
                pack[q][owner, slot] = mine[q][source_tab[owner * SLOTS + slot]]
            return 0

        lax.fori_loop(0, ny, fill, 0)
        spot = held.at[:, :, me_y, :, pl.ds(q * w, w)]
        pltpu.make_async_copy(pack[q].at[me_y], spot, b_recv.at[q]).start()

        def send_block(d, _, q=q, spot=spot):
            pltpu.make_async_remote_copy(
                pack[q].at[peer_y(d)], spot,
                b_send.at[q], b_recv.at[q], (me_x, peer_y(d)), MESH,
            ).start()
            return 0

        lax.fori_loop(1, ny, send_block, 0)

    loads[5].wait()
    loads[6].wait()

    for q in range(q_count):
        landed(held.at[:, :, :, :, pl.ds(q * w, w)], b_recv.at[q])

        def from_left(slot, _, q=q):
            half[slot, :, chunk(q)] = jnp.dot(
                lroot[slot], held[slot, :, :, :, chunk(q)].reshape(blk, w),
                preferred_element_type=F32,
            ).astype(BF16)
            return 0

        lax.fori_loop(0, SLOTS, from_left, 0)

    parts = 4
    part = blk // parts

    def from_right(slot, _):
        squares = jnp.zeros((1, blk), F32)
        for p in range(parts):
            product = jnp.dot(
                half[slot, p * part:(p + 1) * part, :], rroot[slot], preferred_element_type=F32
            )
            direction[p * part:(p + 1) * part, :] = product
            squares = squares + jnp.sum(product * product, axis=0, keepdims=True)
        scale = lax.rsqrt(jnp.sum(squares) / (blk * blk) + EPSILON)
        for q in range(q_count):
            scaled = (direction[:, chunk(q)] * scale).astype(BF16)
            send[q][slot] = scaled.reshape(fold, ny, rows, w)
        return 0

    lax.fori_loop(0, SLOTS, from_right, 0)

    my_slots = pl.ds(me_y * SLOTS, SLOTS)
    for q in range(q_count):
        pltpu.make_async_copy(send[q].at[:, :, me_y], back[q].at[my_slots], c_recv.at[q]).start()

        def send_back(d, _, q=q):
            pltpu.make_async_remote_copy(
                send[q].at[:, :, peer_y(d)], back[q].at[my_slots],
                c_send.at[q], c_recv.at[q], (me_x, peer_y(d)), MESH,
            ).start()
            return 0

        lax.fori_loop(1, ny, send_back, 0)

    loads[7].wait()
    loads[8].wait()

    def statistics(slot, _):
        occupied = slot < owned
        old = jnp.where(occupied, BETA_TWO, 1.0)
        new = jnp.where(occupied, 1.0 - BETA_TWO, 0.0)
        block = held[slot].reshape(blk, blk)
        for p in range(parts):
            at = slice(p * part, (p + 1) * part)
            strip = held[slot, p * fold // parts, (p * part // rows) % ny:][:part // rows].reshape(part, blk)
            gram = lax.dot_general(
                strip, block, (((1,), (1,)), ((), ())), preferred_element_type=F32
            )
            left[slot, at, :] = old * left[slot, at, :] + new * gram
            gram = lax.dot_general(
                held[slot, :, :, :, at].reshape(blk, part), block, (((0,), (0,)), ((), ())),
                preferred_element_type=F32,
            )
            right[slot, at, :] = old * right[slot, at, :] + new * gram
        return 0

    lax.fori_loop(0, SLOTS, statistics, 0)
    kept = [
        pltpu.make_async_copy(left, left_out, keep_sem.at[0]),
        pltpu.make_async_copy(right, right_out, keep_sem.at[1]),
    ]
    for copy in kept:
        copy.start()

    for q in range(q_count):
        landed(back[q], c_recv.at[q])
        for e in range(entries):
            r, block = e // BCOL, e % BCOL
            strips[q][r * fold:(r + 1) * fold, block] = back[q][key_tab[e]]
        pltpu.make_async_copy(strips[q].at[me_x], rows_out.at[q, me_x], d_recv.at[q]).start()

        def send_rows(d, _, q=q):
            pltpu.make_async_remote_copy(
                strips[q].at[peer_x(d)], rows_out.at[q, me_x],
                d_send.at[q], d_recv.at[q], (peer_x(d), me_y), MESH,
            ).start()
            return 0

        lax.fori_loop(1, nx, send_rows, 0)

    for q in range(q_count):
        landed(rows_out.at[q], d_recv.at[q])
        landed(acc[q].at[pl.ds(0, nx - 1)], a_send.at[q])
        landed(pack[q].at[pl.ds(0, ny - 1)], b_send.at[q])
        landed(pack[q].at[pl.ds(0, ny - 1)], c_send.at[q])
        landed(strips[q].at[pl.ds(0, nx - 1)], d_send.at[q])
    landed(xs.at[pl.ds(0, nx - 1)], x_send)
    landed(dys.at[:, pl.ds(0, (ny - 1) * dcols)], dy_send)
    for copy in kept:
        copy.wait()


def finish_kernel(rows_ref, left_ref, right_ref, update_out, left_out, right_out, wide, sems, out_sem):
    copies = [
        pltpu.make_async_copy(left_ref, left_out, sems.at[0]),
        pltpu.make_async_copy(right_ref, right_out, sems.at[1]),
    ]
    for copy in copies:
        copy.start()
    q_count, groups, blocks, _, w = rows_ref.shape
    span = blocks * q_count * w
    for group in range(groups):
        for b in range(blocks):
            for q in range(q_count):
                at = ((group * blocks + b) * q_count + q) * w
                wide[:, at:at + w] = rows_ref[q, group, b].astype(F32)
        at = pl.ds(group * span, span)
        copies.append(pltpu.make_async_copy(wide.at[:, at], update_out.at[:, at], out_sem.at[group]))
        copies[-1].start()
    for copy in copies:
        copy.wait()


def body(
    x_tokens, dy_tokens, samples, grad_acc, owners, left_stats, right_stats, left_roots, right_roots
):
    nx, ny = lax.axis_size("gx"), lax.axis_size("gy")
    rows, cols = grad_acc.shape
    fold = nx // ny
    blk = left_stats.shape[-1]
    q_count = CHUNKS
    w = blk // q_count
    count = samples.shape[0]
    br = ny
    dcols = dy_tokens.shape[1]
    vmem, hbm = pl.BlockSpec(memory_space=pltpu.VMEM), pl.BlockSpec(memory_space=pltpu.HBM)
    anywhere = pl.BlockSpec(memory_space=pl.ANY)

    def each(shape, dtype):
        return [pltpu.VMEM(shape, dtype) for _ in range(q_count)]

    dma = pltpu.SemaphoreType.DMA
    square = (SLOTS, blk, blk)
    rows_back, new_left, new_right = pl.pallas_call(
        functools.partial(exchange_kernel, nx, ny, q_count),
        out_shape=(
            pltpu.VMEM((q_count, nx, BCOL, rows, w), BF16),
            pltpu.VMEM(square, F32),
            pltpu.VMEM(square, F32),
        ),
        in_specs=[hbm] * 9,
        out_specs=(anywhere,) * 3,
        scratch_shapes=[
            *each((nx, BCOL, rows, w), BF16),
            *each((nx, BCOL, rows, w), BF16),
            *each((BCOL * br, fold, rows, w), BF16),
            *each((ny, SLOTS, fold, rows, w), BF16),
            *each((SLOTS, fold, ny, rows, w), BF16),
            *each((ny * SLOTS, fold, rows, w), BF16),
            *each((nx, BCOL, rows, w), BF16),
            pltpu.VMEM((SLOTS, fold, ny, rows, blk), BF16),
            pltpu.VMEM((nx, rows, count), BF16),
            pltpu.VMEM((count, ny * dcols), BF16),
            pltpu.VMEM(square, BF16),
            pltpu.VMEM(square, BF16),
            pltpu.VMEM(square, BF16),
            pltpu.VMEM((blk, blk), F32),
            pltpu.VMEM(square, F32),
            pltpu.VMEM(square, F32),
            pltpu.VMEM(x_tokens.shape, BF16),
            pltpu.VMEM(dy_tokens.shape, BF16),
            pltpu.VMEM((1, count), jnp.int32),
            pltpu.VMEM((rows, cols), F32),
            pltpu.SMEM(owners.shape, jnp.int32),
            pltpu.SMEM((ny * SLOTS,), jnp.int32),
            pltpu.SMEM((br * BCOL,), jnp.int32),
            dma((9,)), dma, dma, dma, dma, dma((2,)),
            *[dma((q_count,)) for _ in range(8)],
        ],
        compiler_params=pltpu.CompilerParams(
            collective_id=0, has_side_effects=True, vmem_limit_bytes=40 * 2**20
        ),
        name="exchange",
    )(*[
        pltpu.with_memory_space_constraint(array, pltpu.HBM)
        for array in (
            x_tokens, dy_tokens, samples.reshape(1, count), grad_acc, owners,
            left_stats[0], right_stats[0], left_roots[0], right_roots[0],
        )
    ])
    update, new_left, new_right = pl.pallas_call(
        finish_kernel,
        out_shape=(
            jax.ShapeDtypeStruct((rows, cols), F32),
            jax.ShapeDtypeStruct(square, F32),
            jax.ShapeDtypeStruct(square, F32),
        ),
        in_specs=[vmem, anywhere, anywhere],
        out_specs=(hbm,) * 3,
        scratch_shapes=[pltpu.VMEM((rows, cols), F32), dma((2,)), dma((nx,))],
        compiler_params=pltpu.CompilerParams(vmem_limit_bytes=16 * 2**20),
        name="finish",
    )(rows_back, new_left, new_right)
    return update, new_left[None], new_right[None]


def solution(mesh):
    split = P(("gx", "gy"), None)
    deep = P(("gx", "gy"), None, None, None)
    return jax.shard_map(
        body,
        mesh=mesh,
        in_specs=(split, P(None, ("gx", "gy")), P(), split, P(), deep, deep, deep, deep),
        out_specs=(split, deep, deep),
        check_vma=False,
    )
```

time: 97.7 us -> 81.4 us (0.83)
  Pallas kernels: 91.9 us -> 80.6 us
  local copies, waits for them, and re-layouts: 4.74 us -> 0 us
    pallas_call x1, Pallas kernels: 10.7 us -> 4.05 us  [body(): pl.pallas_call(finish_kernel, out_shape=(jax.ShapeDtypeStruct((rows, cols...]
    unnamed x10 -> x0, local copies, waits for them, and re-layouts: 4.74 us -> none
    pallas_call x1, Pallas kernels: 81.2 us -> 76.6 us  [body(): pl.pallas_call(functools.partial(exchange_kernel, nx, ny, q_count), out_s...]
where the time goes in v2:
time: 81.4 us; the launch traced here: 81.3 us
  Pallas kernels  80.6 us (99%)
    pallas_call x1, Pallas kernels, body(): pl.pallas_call(functools.partial(exchange_kernel, nx, ny, q_count), out_s...  76.6 us
    pallas_call x1, Pallas kernels, body(): pl.pallas_call(finish_kernel, out_shape=(jax.ShapeDtypeStruct((rows, cols...  4.05 us

profile of v2, /device:TPU:1, one launch (start us, length us, event | category | flops | bytes accessed | tf_op | source)
XLA Modules:
  0.0 81.3 jit_solution(271907643440475525)
XLA Ops:
  0.6 76.6 %exchange.1 = (bf16[4,16,2,32,128]{4,3,2,1,0:T(8,128)(2,1)S(1)}, f32[4,512,512]{2,1,0:T(8,128)S(1)}, f32[4,512,512]{2,1,0:T(8,128)S(1)}) custom-call(bf16[32,1024]{1,0:T(8,128)(2,1)} %x_hbm.1, bf16[1024,128]{1,0:T(8,128)(2,1)} %dy_hbm.1, s32[1,256]{1,0:T(1,128)} %bitcast.11, f32[32,16384]{1,0:T(8,128)} %grad_hbm.1, s32[8,32]{1,0:T(8,128)} %owners_hbm.1, ...), custom_call_target="tpu_custom_call" | custom-call | tf_op jit(solution)/shard_map/exchange/pallas_call | solution.py:336
  77.2 4.0 %finish.1 = (f32[32,16384]{1,0:T(8,128)}, f32[4,512,512]{2,1,0:T(8,128)}, f32[4,512,512]{2,1,0:T(8,128)}) custom-call(bf16[4,16,2,32,128]{4,3,2,1,0:T(8,128)(2,1)S(1)} %get-tuple-element.9.rows_ref, f32[4,512,512]{2,1,0:T(8,128)S(1)} %get-tuple-element.10.left_ref, f32[4,512,512]{2,1,0:T(8,128)S(1)} %get-tuple-element.11.right_ref), custom_call_target="tpu_custom_call" | custom-call | tf_op jit(solution)/shard_map/finish/pallas_call | solution.py:383

commit v3 on v2

v3 whole, which is shorter than its diff:
```python
import functools
import math

import jax
import jax.numpy as jnp
from jax import lax
from jax.experimental import pallas as pl
from jax.experimental.pallas import tpu as pltpu
from jax.sharding import PartitionSpec as P

BCOL = 2
SLOTS = 4
BETA_TWO = 0.9
EPSILON = 1e-06
COLUMNS = 4
FORWARD = ((0, 0, 1), (1, 0, 1), (2, 0, 1), (3, 0, 1))
LEAVE = (((0, 0),), ((0, 1), (1, 0)), ((0, 2),), ((0, 3), (1, 1), (1, 2), (1, 3)))
GROUPS = 2
BACKWARD = ((0, 0, 1), (1, 0, 1), (2, 0, 1), (3, 0, 2), (3, 1, 2))

MESH = pl.DeviceIdType.MESH
F32 = jnp.float32
BF16 = jnp.bfloat16


def cut(chunk, rows, w):
    column, part, parts = chunk
    height = rows // parts
    return column, height, pl.ds(part * height, height), pl.ds(column * w, w)


def exchange_kernel(
    nx, ny, columns, forward, backward,
    x_hbm, dy_hbm, samples_hbm, grad_hbm, owners_hbm, left_hbm, right_hbm, lroot_hbm, rroot_hbm,
    *scratch,
):
    names = iter(scratch)

    def several(count):
        return [next(names) for _ in range(count)]

    ahead, home = len(forward), len(backward)
    rows_out = several(home)
    left_out, right_out = several(2)
    mine_rows = several(ahead)
    acc = several(ahead)
    mine = several(ahead)
    pack = several(ahead)
    landing = several(ahead)
    send = several(home)
    back = several(home)
    strips = several(home)
    (held, xs, dys, lroot, rroot, half, direction, left, right,
     x_ref, dy_ref, samples_ref, grad_ref, owners_ref, source_tab, key_tab) = several(16)
    (ready, in_sem, x_send, x_recv, dy_send, dy_recv, keep_sem,
     a_send, a_recv, b_send, b_recv, c_send, c_recv, d_send, d_recv) = several(15)

    me_x, me_y = lax.axis_index("gx"), lax.axis_index("gy")
    fold = nx // ny
    rows = grad_ref.shape[0]
    blk = fold * ny * rows
    w = blk // columns
    br = ny
    tile = BCOL * blk
    dcols = dy_ref.shape[1]
    entries = br * BCOL
    span = SLOTS // GROUPS
    side = math.isqrt(nx)
    up, across = me_x // side, lax.rem(me_x, side)

    def peer_x(d, e):
        return lax.rem(up + d, side) * side + lax.rem(across + e, side)

    def peer_y(d):
        return lax.rem(me_y + d, ny)

    straight = [peer_x(*d) for n in range(1, side) for d in ((n, 0), (0, n))]
    diagonal = [peer_x(m, n) for m in range(1, side) for n in range(1, side)]
    others = [peer_y(n) for n in range(1, ny)]

    def for_straight(act):
        for gx in straight:
            act(gx)

    def for_diagonal(act):
        for gx in diagonal:
            act(gx)

    def for_y(act):
        for gy in others:
            act(gy)

    barrier = pltpu.get_barrier_semaphore()

    def greet(gx, gy):
        pl.semaphore_signal(barrier, inc=1, device_id=(gx, gy), device_id_type=MESH)

    for_straight(lambda gx: greet(gx, me_y))
    for_y(lambda gy: greet(me_x, gy))

    pairs = [
        (samples_hbm, samples_ref), (x_hbm, x_ref), (dy_hbm, dy_ref), (grad_hbm, grad_ref),
        (owners_hbm, owners_ref), (lroot_hbm, lroot), (rroot_hbm, rroot),
        (left_hbm, left), (right_hbm, right),
    ]
    loads = [pltpu.make_async_copy(a, b, in_sem.at[i]) for i, (a, b) in enumerate(pairs)]
    for load in loads[:5]:
        load.start()
    for load in loads[:3]:
        load.wait()
    pool = x_ref.shape[1]
    count = samples_ref.shape[1]
    chosen = (lax.broadcasted_iota(jnp.int32, (pool, count), 0) == samples_ref[...])
    chosen = jnp.where(chosen, 1.0, 0.0).astype(BF16)
    xs[pl.ds(me_x, 1)] = jnp.dot(x_ref[...], chosen, preferred_element_type=F32).astype(BF16)[None]
    dys[pl.ds(me_y, 1)] = lax.dot_general(
        chosen, dy_ref[...], (((0,), (0,)), ((), ())), preferred_element_type=F32
    ).astype(BF16)[None]
    loads[3].wait()

    def narrow(group, _):
        for i, chunk in enumerate(forward):
            column, _, its_rows, _ = cut(chunk, rows, w)
            for block in range(BCOL):
                first = pl.multiple_of(group * tile + block * blk + column * w, 128)
                mine_rows[i][group, block] = grad_ref[its_rows, pl.ds(first, w)].astype(BF16)
        return 0

    lax.fori_loop(0, nx, narrow, 0)

    def send_x(gx):
        pltpu.make_async_remote_copy(
            xs.at[me_x], xs.at[me_x], x_send, x_recv, (gx, me_y), MESH
        ).start()

    def send_dy(gy):
        pltpu.make_async_remote_copy(
            dys.at[me_y], dys.at[me_y], dy_send, dy_recv, (me_x, gy), MESH
        ).start()

    def send_acc(i):
        def act(gx):
            pltpu.make_async_remote_copy(
                mine_rows[i].at[gx], acc[i].at[me_x], a_send.at[i], a_recv.at[i], (gx, me_y), MESH
            ).start()

        return act

    def vouch(d, _):
        pl.semaphore_signal(ready, inc=1, device_id=(peer_x(0, d), me_y), device_id_type=MESH)
        return 0

    pl.semaphore_wait(barrier, 2 * (side - 1) + ny - 1)
    lax.fori_loop(1, side, vouch, 0)
    for_straight(send_x)
    for_y(send_dy)
    for_straight(send_acc(0))
    pl.semaphore_wait(ready, side - 1)
    for_diagonal(send_x)
    for_diagonal(send_acc(0))
    for i in range(ahead):
        pltpu.make_async_copy(mine_rows[i].at[me_x], acc[i].at[me_x], a_recv.at[i]).start()
        if i:
            for_straight(send_acc(i))
            for_diagonal(send_acc(i))

    for load in loads[5:]:
        load.start()

    loads[4].wait()
    keys = []
    owned = jnp.int32(0)
    listed = [owners_ref[e // BCOL, me_x * BCOL + e % BCOL] for e in range(entries)]
    for e in range(entries):
        rank = jnp.int32(0)
        for before in range(e):
            rank = rank + jnp.where(listed[before] == listed[e], 1, 0)
        keys.append(listed[e] * SLOTS + rank)
        key_tab[e] = keys[e]
        owned = owned + jnp.where(listed[e] == me_y, 1, 0)

    def find_source(k, _):
        place = jnp.int32(0)
        for e in range(entries):
            place = place + jnp.where(keys[e] == k, (e % BCOL) * br + e // BCOL, 0)
        source_tab[k] = place
        return 0

    lax.fori_loop(0, ny * SLOTS, find_source, 0)

    def landed(ref, sem):
        pltpu.make_async_copy(ref, ref, sem).wait()

    def picked(first):
        if dcols >= w:
            return dys[first // dcols, :, first % dcols:first % dcols + w]
        return jnp.concatenate([dys[j] for j in range(first // dcols, (first + w) // dcols)], axis=1)

    for i, chunk in enumerate(forward):
        column, height, its_rows, its_columns = cut(chunk, rows, w)
        if i == 0:
            landed(xs.at[pl.ds(0, nx - 1)], x_recv)
            landed(dys.at[pl.ds(0, ny - 1)], dy_recv)
        landed(acc[i], a_recv.at[i])
        for block in range(BCOL):
            product = jnp.dot(
                xs[:, its_rows, :].reshape(nx * height, count),
                picked(block * blk + column * w),
                preferred_element_type=F32,
            ).reshape(nx, height, w)
            total = (acc[i][:, block].astype(F32) + product).astype(BF16)
            mine[i][block * br:(block + 1) * br] = total.reshape(br, fold, height, w)

        def fill(owner, _, i=i):
            for slot in range(SLOTS):
                pack[i][owner, slot] = mine[i][source_tab[owner * SLOTS + slot]]
            return 0

        lax.fori_loop(0, ny, fill, 0)
        for group, k in LEAVE[i]:
            its_slots = pl.ds(group * span, span)
            spot = landing[k].at[me_y, its_slots]
            pltpu.make_async_copy(pack[k].at[me_y, its_slots], spot, b_recv.at[group, k]).start()

            def send_block(gy, group=group, k=k, spot=spot, its_slots=its_slots):
                pltpu.make_async_remote_copy(
                    pack[k].at[gy, its_slots], spot,
                    b_send.at[group, k], b_recv.at[group, k], (me_x, gy), MESH,
                ).start()

            for_y(send_block)

    loads[5].wait()
    loads[6].wait()

    parts = 4
    part = blk // parts
    bands = part // rows

    def from_right(slot, _):
        squares = jnp.zeros((1, blk), F32)
        for p in range(parts):
            product = jnp.dot(
                half[slot, p * part:(p + 1) * part, :], rroot[slot], preferred_element_type=F32
            )
            direction[p * part:(p + 1) * part, :] = product
            squares = squares + jnp.sum(product * product, axis=0, keepdims=True)
        scale = lax.rsqrt(jnp.sum(squares) / (blk * blk) + EPSILON)
        for i, chunk in enumerate(backward):
            column, height, its_rows, its_columns = cut(chunk, rows, w)
            begin = chunk[1] * height
            scaled = (direction[:, its_columns] * scale).astype(BF16).reshape(fold, ny, rows, w)
            for f in range(fold):
                send[i][:, slot, f] = scaled[f, :, begin:begin + height, :]
        return 0

    def statistics(slot, _):
        occupied = slot < owned
        old = jnp.where(occupied, BETA_TWO, 1.0)
        new = jnp.where(occupied, 1.0 - BETA_TWO, 0.0)
        block = held[slot].reshape(blk, blk)
        for p in range(parts):
            at = slice(p * part, (p + 1) * part)
            first = p * bands % ny
            strip = held[slot, p * bands // ny, first:first + bands].reshape(part, blk)
            gram = lax.dot_general(
                strip, block, (((1,), (1,)), ((), ())), preferred_element_type=F32
            )
            left[slot, at, :] = old * left[slot, at, :] + new * gram
            gram = lax.dot_general(
                held[slot, :, :, :, at].reshape(blk, part), block, (((0,), (0,)), ((), ())),
                preferred_element_type=F32,
            )
            right[slot, at, :] = old * right[slot, at, :] + new * gram
        return 0

    for group in range(GROUPS):
        first = group * span
        its_slots = pl.ds(first, span)
        for i, chunk in enumerate(forward):
            _, _, its_rows, its_columns = cut(chunk, rows, w)
            landed(landing[i].at[:, its_slots], b_recv.at[group, i])
            for slot in range(first, first + span):
                for f in range(fold):
                    held[slot, f, :, its_rows, its_columns] = landing[i][:, slot, f]

            def from_left(slot, _, its_columns=its_columns):
                half[slot, :, its_columns] = jnp.dot(
                    lroot[slot], held[slot, :, :, :, its_columns].reshape(blk, w),
                    preferred_element_type=F32,
                ).astype(BF16)
                return 0

            lax.fori_loop(first, first + span, from_left, 0)
        lax.fori_loop(first, first + span, from_right, 0)
        my_slots = pl.ds(me_y * SLOTS + first, span)
        for i in range(home):
            spot = back[i].at[my_slots]
            pltpu.make_async_copy(send[i].at[me_y, its_slots], spot, c_recv.at[group, i]).start()

            def send_back(gy, i=i, group=group, spot=spot, its_slots=its_slots):
                pltpu.make_async_remote_copy(
                    send[i].at[gy, its_slots], spot,
                    c_send.at[group, i], c_recv.at[group, i], (me_x, gy), MESH,
                ).start()

            for_y(send_back)

        if group == 0:
            loads[7].wait()
            loads[8].wait()
        lax.fori_loop(first, first + span, statistics, 0)

    kept = [
        pltpu.make_async_copy(left, left_out, keep_sem.at[0]),
        pltpu.make_async_copy(right, right_out, keep_sem.at[1]),
    ]
    for copy in kept:
        copy.start()

    def for_x(act):
        for_straight(act)
        for_diagonal(act)

    for i in range(home):
        for group in range(GROUPS):
            landed(back[i].at[pl.ds(0, ny * span)], c_recv.at[group, i])
        for e in range(entries):
            r, block = e // BCOL, e % BCOL
            strips[i][r * fold:(r + 1) * fold, block] = back[i][key_tab[e]]
        spot = rows_out[i].at[me_x]
        pltpu.make_async_copy(strips[i].at[me_x], spot, d_recv.at[i]).start()

        def send_rows(gx, i=i, spot=spot):
            pltpu.make_async_remote_copy(
                strips[i].at[gx], spot, d_send.at[i], d_recv.at[i], (gx, me_y), MESH
            ).start()

        for_x(send_rows)

    for i in range(home):
        landed(rows_out[i], d_recv.at[i])
    for i in range(ahead):
        landed(acc[i].at[pl.ds(0, nx - 1)], a_send.at[i])
        for group in range(GROUPS):
            landed(pack[i].at[pl.ds(0, ny - 1), pl.ds(0, span)], b_send.at[group, i])
    for i in range(home):
        for group in range(GROUPS):
            landed(back[i].at[pl.ds(0, (ny - 1) * span)], c_send.at[group, i])
        landed(strips[i].at[pl.ds(0, nx - 1)], d_send.at[i])
    landed(xs.at[pl.ds(0, nx - 1)], x_send)
    landed(dys.at[pl.ds(0, ny - 1)], dy_send)
    for copy in kept:
        copy.wait()


def finish_kernel(chunks, *refs):
    rows_refs = refs[:len(chunks)]
    left_ref, right_ref, update_out, left_out, right_out, wide, sems, out_sem = refs[len(chunks):]
    copies = [
        pltpu.make_async_copy(left_ref, left_out, sems.at[0]),
        pltpu.make_async_copy(right_ref, right_out, sems.at[1]),
    ]
    for copy in copies:
        copy.start()
    rows = wide.shape[0]
    groups, blocks, _, w = rows_refs[0].shape
    blk = wide.shape[1] // (groups * blocks)
    for group in range(groups):
        for b in range(blocks):
            for ref, chunk in zip(rows_refs, chunks):
                column, height, its_rows, _ = cut(chunk, rows, w)
                at = (group * blocks + b) * blk + column * w
                wide[its_rows, at:at + w] = ref[group, b].astype(F32)
        at = pl.ds(group * blocks * blk, blocks * blk)
        copies.append(pltpu.make_async_copy(wide.at[:, at], update_out.at[:, at], out_sem.at[group]))
        copies[-1].start()
    for copy in copies:
        copy.wait()


def body(
    x_tokens, dy_tokens, samples, grad_acc, owners, left_stats, right_stats, left_roots, right_roots
):
    nx, ny = lax.axis_size("gx"), lax.axis_size("gy")
    rows, cols = grad_acc.shape
    fold = nx // ny
    blk = left_stats.shape[-1]
    w = blk // COLUMNS
    count = samples.shape[0]
    br = ny
    dcols = dy_tokens.shape[1]
    vmem, hbm = pl.BlockSpec(memory_space=pltpu.VMEM), pl.BlockSpec(memory_space=pltpu.HBM)
    anywhere = pl.BlockSpec(memory_space=pl.ANY)

    def each(chunks, *shape):
        heights = [rows // chunk[2] for chunk in chunks]
        return [
            pltpu.VMEM(tuple(h if n is None else n for n in shape), BF16) for h in heights
        ]

    dma = pltpu.SemaphoreType.DMA
    square = (SLOTS, blk, blk)
    *rows_back, new_left, new_right = pl.pallas_call(
        functools.partial(exchange_kernel, nx, ny, COLUMNS, FORWARD, BACKWARD),
        out_shape=(
            *each(BACKWARD, nx, BCOL, None, w),
            pltpu.VMEM(square, F32),
            pltpu.VMEM(square, F32),
        ),
        in_specs=[hbm] * 9,
        out_specs=(anywhere,) * (len(BACKWARD) + 2),
        scratch_shapes=[
            *each(FORWARD, nx, BCOL, None, w),
            *each(FORWARD, nx, BCOL, None, w),
            *each(FORWARD, BCOL * br, fold, None, w),
            *each(FORWARD, ny, SLOTS, fold, None, w),
            *each(FORWARD, ny, SLOTS, fold, None, w),
            *each(BACKWARD, ny, SLOTS, fold, None, w),
            *each(BACKWARD, ny * SLOTS, fold, None, w),
            *each(BACKWARD, nx, BCOL, None, w),
            pltpu.VMEM((SLOTS, fold, ny, rows, blk), BF16),
            pltpu.VMEM((nx, rows, count), BF16),
            pltpu.VMEM((ny, count, dcols), BF16),
            pltpu.VMEM(square, BF16),
            pltpu.VMEM(square, BF16),
            pltpu.VMEM(square, BF16),
            pltpu.VMEM((blk, blk), F32),
            pltpu.VMEM(square, F32),
            pltpu.VMEM(square, F32),
            pltpu.VMEM(x_tokens.shape, BF16),
            pltpu.VMEM(dy_tokens.shape, BF16),
            pltpu.VMEM((1, count), jnp.int32),
            pltpu.VMEM((rows, cols), F32),
            pltpu.SMEM(owners.shape, jnp.int32),
            pltpu.SMEM((ny * SLOTS,), jnp.int32),
            pltpu.SMEM((br * BCOL,), jnp.int32),
            pltpu.SemaphoreType.REGULAR,
            dma((9,)), *[dma] * 4, dma((2,)),
            *[dma((len(FORWARD),))] * 2,
            *[dma((GROUPS, len(FORWARD)))] * 2,
            *[dma((GROUPS, len(BACKWARD)))] * 2,
            *[dma((len(BACKWARD),))] * 2,
        ],
        compiler_params=pltpu.CompilerParams(
            collective_id=0, has_side_effects=True, vmem_limit_bytes=42 * 2**20
        ),
        name="exchange",
    )(*[
        pltpu.with_memory_space_constraint(array, pltpu.HBM)
        for array in (
            x_tokens, dy_tokens, samples.reshape(1, count), grad_acc, owners,
            left_stats[0], right_stats[0], left_roots[0], right_roots[0],
        )
    ])
    update, new_left, new_right = pl.pallas_call(
        functools.partial(finish_kernel, BACKWARD),
        out_shape=(
            jax.ShapeDtypeStruct((rows, cols), F32),
            jax.ShapeDtypeStruct(square, F32),
            jax.ShapeDtypeStruct(square, F32),
        ),
        in_specs=[vmem] * len(BACKWARD) + [anywhere] * 2,
        out_specs=(hbm,) * 3,
        scratch_shapes=[pltpu.VMEM((rows, cols), F32), dma((2,)), dma((nx,))],
        compiler_params=pltpu.CompilerParams(vmem_limit_bytes=12 * 2**20),
        name="finish",
    )(*rows_back, new_left, new_right)
    return update, new_left[None], new_right[None]


def solution(mesh):
    split = P(("gx", "gy"), None)
    deep = P(("gx", "gy"), None, None, None)
    return jax.shard_map(
        body,
        mesh=mesh,
        in_specs=(split, P(None, ("gx", "gy")), P(), split, P(), deep, deep, deep, deep),
        out_specs=(split, deep, deep),
        check_vma=False,
    )
```

time: 81.4 us -> 78.9 us (0.969)
  Pallas kernels: 80.6 us -> 78.1 us
    pallas_call x2, Pallas kernels: 80.6 us -> 78.1 us  [the longest x1 74.1 us: body(): pl.pallas_call(functools.partial(exchange_kernel, nx, ny, COLUMNS, FORWAR...]
where the time goes in v3:
time: 78.9 us; the launch traced here: 78.8 us
  Pallas kernels  78.1 us (99%)
    pallas_call x1, Pallas kernels, body(): pl.pallas_call(functools.partial(exchange_kernel, nx, ny, COLUMNS, FORWAR...  74.1 us
    pallas_call x1, Pallas kernels, body(): pl.pallas_call(functools.partial(finish_kernel, BACKWARD), out_shape=(jax...  4.06 us

profile of v3, /device:TPU:1, one launch (start us, length us, event | category | flops | bytes accessed | tf_op | source)
XLA Modules:
  0.0 78.8 jit_solution(11310604237175429812)
XLA Ops:
  0.6 74.1 %exchange.1 = (bf16[16,2,32,128]{3,2,1,0:T(8,128)(2,1)S(1)}, bf16[16,2,32,128]{3,2,1,0:T(8,128)(2,1)S(1)}, bf16[16,2,32,128]{3,2,1,0:T(8,128)(2,1)S(1)}, bf16[16...) custom-call(bf16[32,1024]{1,0:T(8,128)(2,1)} %x_hbm.1, ...), custom_call_target="tpu_custom_call" | custom-call | tf_op jit(solution)/shard_map/exchange/pallas_call | solution.py:404
  74.7 4.1 %finish.1 = (f32[32,16384]{1,0:T(8,128)}, f32[4,512,512]{2,1,0:T(8,128)}, f32[4,512,512]{2,1,0:T(8,128)}) custom-call(bf16[16,2,32,128]{3,2,1,0:T(8,128)(2,1)S(1)} %get-tuple-element.13.refs_0_, bf16[16,2,32,128]{3,2,1,0:T(8,128)(2,1)S(1)} %get-tuple-element.14.refs_1_, bf16[16,2,32,128]{3,2,1,0:T(8,128)(2,1)S(1)} %get-tuple-element.15.refs_2_, ...), custom_call_target="tpu_custom_call" | custom-call | tf_op jit(solution)/shard_map/finish/pallas_call | solution.py:456

commit v4 on v3

--- a/solution.py
+++ b/solution.py
@@ -14,8 +14,9 @@
 EPSILON = 1e-06
 COLUMNS = 4
 FORWARD = ((0, 0, 1), (1, 0, 1), (2, 0, 1), (3, 0, 1))
-LEAVE = (((0, 0),), ((0, 1), (1, 0)), ((0, 2),), ((0, 3), (1, 1), (1, 2), (1, 3)))
+LEAVE = (((0, 0), (1, 0)), ((0, 1),), ((0, 2),), ((0, 3), (1, 1), (1, 2), (1, 3)))
 GROUPS = 2
+FIRST = 3
 BACKWARD = ((0, 0, 1), (1, 0, 1), (2, 0, 1), (3, 0, 2), (3, 1, 2))
 
 MESH = pl.DeviceIdType.MESH
@@ -274,6 +275,22 @@
             right[slot, at, :] = old * right[slot, at, :] + new * gram
         return 0
 
+    def send_back(group, i):
+        its_slots = pl.ds(group * span, span)
+        spot = back[i].at[pl.ds(me_y * SLOTS + group * span, span)]
+        pltpu.make_async_copy(send[i].at[me_y, its_slots], spot, c_recv.at[group, i]).start()
+
+        def act(gy):
+            pltpu.make_async_remote_copy(
+                send[i].at[gy, its_slots], spot,
+                c_send.at[group, i], c_recv.at[group, i], (me_x, gy), MESH,
+            ).start()
+
+        for_y(act)
+
+    def sent_back(group, i):
+        landed(back[i].at[pl.ds(0, (ny - 1) * span)], c_send.at[group, i])
+
     for group in range(GROUPS):
         first = group * span
         its_slots = pl.ds(first, span)
@@ -293,24 +310,16 @@
 
             lax.fori_loop(first, first + span, from_left, 0)
         lax.fori_loop(first, first + span, from_right, 0)
-        my_slots = pl.ds(me_y * SLOTS + first, span)
-        for i in range(home):
-            spot = back[i].at[my_slots]
-            pltpu.make_async_copy(send[i].at[me_y, its_slots], spot, c_recv.at[group, i]).start()
-
-            def send_back(gy, i=i, group=group, spot=spot, its_slots=its_slots):
-                pltpu.make_async_remote_copy(
-                    send[i].at[gy, its_slots], spot,
-                    c_send.at[group, i], c_recv.at[group, i], (me_x, gy), MESH,
-                ).start()
-
-            for_y(send_back)
-
+        for i in range(FIRST):
+            send_back(group, i)
         if group == 0:
             loads[7].wait()
             loads[8].wait()
         lax.fori_loop(first, first + span, statistics, 0)
 
+    for i in range(FIRST, home):
+        for group in range(GROUPS):
+            send_back(group, i)
     kept = [
         pltpu.make_async_copy(left, left_out, keep_sem.at[0]),
         pltpu.make_async_copy(right, right_out, keep_sem.at[1]),
@@ -346,7 +355,7 @@
             landed(pack[i].at[pl.ds(0, ny - 1), pl.ds(0, span)], b_send.at[group, i])
     for i in range(home):
         for group in range(GROUPS):
-            landed(back[i].at[pl.ds(0, (ny - 1) * span)], c_send.at[group, i])
+            sent_back(group, i)
         landed(strips[i].at[pl.ds(0, nx - 1)], d_send.at[i])
     landed(xs.at[pl.ds(0, nx - 1)], x_send)
     landed(dys.at[pl.ds(0, ny - 1)], dy_send)

time: 78.9 us -> 74.5 us (0.944)
  Pallas kernels: 78.1 us -> 73.7 us
    pallas_call x1, Pallas kernels: 74.1 us -> 69.6 us  [body(): pl.pallas_call(functools.partial(exchange_kernel, nx, ny, COLUMNS, FORWAR...]
where the time goes in v4:
time: 74.5 us; the launch traced here: 74.3 us
  Pallas kernels  73.7 us (99%)
    pallas_call x1, Pallas kernels, body(): pl.pallas_call(functools.partial(exchange_kernel, nx, ny, COLUMNS, FORWAR...  69.6 us
    pallas_call x1, Pallas kernels, body(): pl.pallas_call(functools.partial(finish_kernel, BACKWARD), out_shape=(jax...  4.06 us

profile of v4, /device:TPU:1, one launch (start us, length us, event | category | flops | bytes accessed | tf_op | source)
XLA Modules:
  0.0 74.3 jit_solution(15687070725428820177)
XLA Ops:
  0.6 69.6 %exchange.1 = (bf16[16,2,32,128]{3,2,1,0:T(8,128)(2,1)S(1)}, bf16[16,2,32,128]{3,2,1,0:T(8,128)(2,1)S(1)}, bf16[16,2,32,128]{3,2,1,0:T(8,128)(2,1)S(1)}, bf16[16...) custom-call(bf16[32,1024]{1,0:T(8,128)(2,1)} %x_hbm.1, ...), custom_call_target="tpu_custom_call" | custom-call | tf_op jit(solution)/shard_map/exchange/pallas_call | solution.py:413
  70.3 4.1 %finish.1 = (f32[32,16384]{1,0:T(8,128)}, f32[4,512,512]{2,1,0:T(8,128)}, f32[4,512,512]{2,1,0:T(8,128)}) custom-call(bf16[16,2,32,128]{3,2,1,0:T(8,128)(2,1)S(1)} %get-tuple-element.13.refs_0_, bf16[16,2,32,128]{3,2,1,0:T(8,128)(2,1)S(1)} %get-tuple-element.14.refs_1_, bf16[16,2,32,128]{3,2,1,0:T(8,128)(2,1)S(1)} %get-tuple-element.15.refs_2_, ...), custom_call_target="tpu_custom_call" | custom-call | tf_op jit(solution)/shard_map/finish/pallas_call | solution.py:465

commit v5 on v4

--- a/solution.py
+++ b/solution.py
@@ -16,8 +16,8 @@
 FORWARD = ((0, 0, 1), (1, 0, 1), (2, 0, 1), (3, 0, 1))
 LEAVE = (((0, 0), (1, 0)), ((0, 1),), ((0, 2),), ((0, 3), (1, 1), (1, 2), (1, 3)))
 GROUPS = 2
-FIRST = 3
-BACKWARD = ((0, 0, 1), (1, 0, 1), (2, 0, 1), (3, 0, 2), (3, 1, 2))
+FIRST = 5
+BACKWARD = tuple((column, part, 2) for column in range(COLUMNS) for part in range(2))
 
 MESH = pl.DeviceIdType.MESH
 F32 = jnp.float32
@@ -153,8 +153,8 @@
 
     pl.semaphore_wait(barrier, 2 * (side - 1) + ny - 1)
     lax.fori_loop(1, side, vouch, 0)
+    for_y(send_dy)
     for_straight(send_x)
-    for_y(send_dy)
     for_straight(send_acc(0))
     pl.semaphore_wait(ready, side - 1)
     for_diagonal(send_x)

time: 74.5 us -> 74.4 us (level)
  no operation moved by 1% of the time
where the time goes in v5:
time: 74.4 us; the launch traced here: 74.2 us
  Pallas kernels  73.6 us (99%)
    pallas_call x1, Pallas kernels, body(): pl.pallas_call(functools.partial(exchange_kernel, nx, ny, COLUMNS, FORWAR...  69.5 us
    pallas_call x1, Pallas kernels, body(): pl.pallas_call(functools.partial(finish_kernel, BACKWARD), out_shape=(jax...  4.05 us

profile of v5, /device:TPU:1, one launch (start us, length us, event | category | flops | bytes accessed | tf_op | source)
XLA Modules:
  0.0 74.2 jit_solution(11067111695247299011)
XLA Ops:
  0.6 69.5 %exchange.1 = (bf16[16,2,16,128]{3,2,1,0:T(8,128)(2,1)S(1)}, bf16[16,2,16,128]{3,2,1,0:T(8,128)(2,1)S(1)}, bf16[16,2,16,128]{3,2,1,0:T(8,128)(2,1)S(1)}, bf16[16...) custom-call(bf16[32,1024]{1,0:T(8,128)(2,1)} %x_hbm.1, ...), custom_call_target="tpu_custom_call" | custom-call | tf_op jit(solution)/shard_map/exchange/pallas_call | solution.py:413
  70.2 4.0 %finish.1 = (f32[32,16384]{1,0:T(8,128)}, f32[4,512,512]{2,1,0:T(8,128)}, f32[4,512,512]{2,1,0:T(8,128)}) custom-call(bf16[16,2,16,128]{3,2,1,0:T(8,128)(2,1)S(1)} %get-tuple-element.16.refs_0_, bf16[16,2,16,128]{3,2,1,0:T(8,128)(2,1)S(1)} %get-tuple-element.17.refs_1_, bf16[16,2,16,128]{3,2,1,0:T(8,128)(2,1)S(1)} %get-tuple-element.18.refs_2_, ...), custom_call_target="tpu_custom_call" | custom-call | tf_op jit(solution)/shard_map/finish/pallas_call | solution.py:465
